TPU v7x, 32 devices: a whole 2x2x4 slice. The times are simulated.
32 devices in a mesh: group: 2 (over x), cell: 16 (over z, y, core).
Axes of the slice: x: 2, y: 2, z: 4, core: 2. Of those that a mesh axis runs over, the one named last changes fastest.
Arguments:
- adjoint_seed: float32 [32, 5, 16384], P('group', None, 'cell'), parts along dimension 0, may hold values from -6 to 6
- inv_blocks: bfloat16 [32, 5, 5, 16384], P('group', None, None, 'cell'), parts along dimension 0
- flux_jacobians: float32 [2, 32, 5, 5], P(None, 'group'), parts along dimension 1, may hold values from -1.5 to 1.5
- modal_shapes: float32 [20, 5, 16384], P(None, None, 'cell'), may hold values from -0.01953125 to 0.01953125
- modal_gain: float32 [40], P('group'), parts along dimension 0, may hold values from 0.05 to 0.3
- face_cells: int32 [2, 49152], P(None, 'cell'), may hold values from 0 to 1279, as said below
- face_weights: float32 [49152], P('cell'), may hold values from 0.4 to 1
- colours: int32 [16384], P('cell'), may hold values from 0 to 1
- send_cells: int32 [2, 2048], P(None, 'cell'), may hold values from 0 to 1023, as said below
Outputs:
- adjoint_state: float32 [32, 5, 16384], P('group', None, 'cell'), parts along dimension 0
- modal_partials: float32 [32, 20], P('group'), parts along dimension 0
There are 2 independent parts, one for each index of `group`. A program takes and returns all parts, laid end to end along the dimension named above; an argument that names none is the same for every part. Nothing has to cross between parts.
Inputs may be any that keep to these rules, and one draw needn't show every extreme that they name: `face_cells`: each face's left cell is a local cell or a lower ghost (from 1024 to 1151); its right cell is a local cell or an upper ghost (from 1152 on). `send_cells`: within a partition the 256 listed cells are distinct local cells.
All inputs are finite; a program needn't handle non-finite values.
Results may differ from a plain program's by a relative error of at most 0.0003.
Values sent between devices are 32-bit elements; how exact they have to be, the bound alone decides.
A program may use at most 64 MiB of HBM per device.

v0:
```python
import math
import jax
import jax.numpy as jnp
import numpy as np
from jax import lax
from jax.sharding import PartitionSpec as P

ITERS = 4
frequency = 0.04


def from_behind(value, axis, by):
    devices = lax.axis_size(axis)
    return lax.ppermute(value, axis, [(i, (i + by) % devices) for i in range(devices)])


def spectral_matrix(count):
    index = jnp.arange(count)
    apart = index[:, None] - index[None, :]
    angle = math.pi * apart.astype(jnp.float32) / count
    parity = jnp.where(apart % 2 == 0, 1.0, -1.0).astype(jnp.float32)
    safe_sin = jnp.where(apart == 0, 1.0, jnp.sin(angle))
    return jnp.where(apart == 0, 0.0, 0.5 * parity * jnp.cos(angle) / safe_sin)


def wide_dot(left, right):
    return jnp.dot(left, right, precision=lax.Precision.HIGHEST, preferred_element_type=jnp.float32)


def modal_total(state_rows, shape_rows, count, nvar, modes):
    gram = lax.dot_general(
        state_rows,
        shape_rows,
        (((1,), (1,)), ((), ())),
        precision=lax.Precision.HIGHEST,
        preferred_element_type=jnp.float32,
    )
    local_part = jnp.einsum("ivmv->im", gram.reshape(count, nvar, modes, nvar))
    return lax.psum(local_part, "cell")


def local(
    adjoint_seed,
    inv_blocks,
    flux_jacobians,
    modal_shapes,
    modal_gain,
    face_cells,
    face_weights,
    colours,
    send_cells,
):
    count, nvar, owned = adjoint_seed.shape
    modes = modal_shapes.shape[0]
    rows = count * nvar
    eye_inst = jnp.eye(count, dtype=jnp.float32)
    eye_var = jnp.eye(nvar, dtype=jnp.float32)
    left_matrix = jnp.einsum("ij,ivw->iwjv", eye_inst, flux_jacobians[0]).reshape(rows, rows)
    right_matrix = jnp.einsum("ij,ivw->iwjv", eye_inst, flux_jacobians[1]).reshape(rows, rows)
    spectral = spectral_matrix(count)
    spectral_rows = frequency * jnp.einsum("jk,vu->kvju", spectral, eye_var).reshape(rows, rows)
    seed_rows = adjoint_seed.reshape(rows, owned)
    shape_rows = modal_shapes.reshape(modes * nvar, owned)
    flat_inverse = inv_blocks.reshape(count * nvar * nvar, owned)
    inst_index = np.arange(count)[:, None]
    out_index = np.arange(nvar)[None, :]
    inverse_parts = []
    source_rows = []
    for var in range(nvar):
        pick = (inst_index * nvar * nvar + var * nvar + out_index).reshape(-1)
        inverse_parts.append(
            jnp.take(flat_inverse, jnp.asarray(pick, jnp.int32), axis=0).astype(jnp.float32)
        )
        source_rows.append(
            jnp.asarray((inst_index * nvar + var + 0 * out_index).reshape(-1), jnp.int32)
        )
    left_cells = face_cells[0]
    right_cells = face_cells[1]
    colour_mask = colours[None, :]
    state = jnp.zeros_like(seed_rows)
    for sweep in range(ITERS):
        lam = modal_total(state, shape_rows, count, nvar, modes) * modal_gain[None, :]
        lift = jnp.einsum("im,vu->ivmu", lam, eye_var).reshape(rows, modes * nvar)
        base = seed_rows + wide_dot(lift, shape_rows)
        to_lower = jnp.take(state, send_cells[0], axis=1)
        to_upper = jnp.take(state, send_cells[1], axis=1)
        from_lower = from_behind(to_upper, "cell", 1)
        from_upper = from_behind(to_lower, "cell", -1)
        ghosts = jnp.concatenate([from_lower, from_upper], axis=1)
        for colour in range(2):
            extended = jnp.concatenate([state, ghosts], axis=1)
            from_left = wide_dot(left_matrix, extended)
            from_right = wide_dot(right_matrix, extended)
            total = jnp.zeros_like(extended)
            total = total.at[:, right_cells].add(
                face_weights * jnp.take(from_left, left_cells, axis=1)
            )
            total = total.at[:, left_cells].add(
                face_weights * jnp.take(from_right, right_cells, axis=1)
            )
            spectral_term = wide_dot(spectral_rows, state)
            resid = base - total[:, :owned] - spectral_term
            updated = inverse_parts[0] * jnp.take(resid, source_rows[0], axis=0)
            for var in range(1, nvar):
                updated = updated + inverse_parts[var] * jnp.take(resid, source_rows[var], axis=0)
            state = jnp.where(colour_mask == colour, updated, state)
    partials = modal_total(state, shape_rows, count, nvar, modes)
    return (state.reshape(count, nvar, owned), partials)


def solution(mesh):
    return jax.shard_map(
        local,
        mesh=mesh,
        in_specs=(
            P("group", None, "cell"),
            P("group", None, None, "cell"),
            P(None, "group", None, None),
            P(None, None, "cell"),
            P("group"),
            P(None, "cell"),
            P("cell"),
            P("cell"),
            P(None, "cell"),
        ),
        out_specs=(P("group", None, "cell"), P("group", None)),
        check_vma=False,
    )
```

profile of v0, /device:TPU:0, one launch (start us, length us, event | category | flops | bytes accessed | tf_op | source)
XLA Modules:
  0.0 821.3 jit_solution(13111969591882598238)
XLA Ops:
  2.9 5.4 collective-permute-start.1
  12.7 34.5 %psum.35 = f32[16,20]{1,0:T(8,128)S(1)} all-reduce(f32[16,20]{1,0:T(8,128)S(1)} %fusion.48), channel_id=1, replica_groups=mesh['group'=2,'cell'=16] {'cell'}, use_global_device_ids=true, to_apply=%region_1.3 | all-reduce | flops 320 | bytes 2560 | tf_op jit(solution)/shard_map/psum | solution.py:39
  65.2 26.8 %scatter_custom_fusion = f32[80,1280]{0,1:T(8,128)} fusion(s32[3072]{0:T(1024)} %bitcast.273, f32[]{:T(128)} %constant.24.clone.8, f32[3072]{0:T(1024)S(1)} %copy-done.1, pred[3072]{0:T(1024)(128)(4,1)S(1)} %compare_and_fusion, f32[]{:T(128)} %constant.44.clone.1, f32[80,1280]{0,1:T(8,128)S(1)} %fusion.107, s32[3072]{0:T(1024)S(1)} %fusion.178), kind=kCustom, calls=%fused_computation.130 | custom fusion | flops 737280 | bytes 847872 | tf_op jit(solution)/shard_map/scatter-add | solution.py:95
  94.0 27.7 %scatter_custom_fusion.1 = f32[80,1280]{0,1:T(8,128)} fusion(f32[80,1280]{0,1:T(8,128)} %scatter_custom_fusion, s32[3072]{0:T(1024)} %bitcast.265, f32[]{:T(128)} %constant.24.clone.8, f32[3072]{0:T(1024)S(1)} %copy-done.1, pred[3072]{0:T(1024)(128)(4,1)S(1)} %compare_and_fusion.1, f32[80,1280]{0,1:T(8,128)S(1)} %fusion.106, s32[3072]{0:T(1024)S(1)} %fusion.177), kind=kCustom, calls=%fused_computation.127 | custom fusion | flops 737280 | bytes 847360 | tf_op jit(solution)/shard_map/scatter-add | solution.py:98
  132.2 26.8 %scatter_custom_fusion.2 = f32[80,1280]{0,1:T(8,128)} fusion(s32[3072]{0:T(1024)} %bitcast.274, f32[]{:T(128)} %constant.24.clone.8, f32[3072]{0:T(1024)S(1)} %copy-done.1, pred[3072]{0:T(1024)(128)(4,1)S(1)} %compare_and_fusion, f32[]{:T(128)} %constant.44.clone.1, f32[80,1280]{0,1:T(8,128)S(1)} %fusion.174, s32[3072]{0:T(1024)S(1)} %fusion.178), kind=kCustom, calls=%fused_computation.124 | custom fusion | flops 737280 | bytes 847872 | tf_op jit(solution)/shard_map/scatter-add | solution.py:95
  161.0 27.7 %scatter_custom_fusion.3 = f32[80,1280]{0,1:T(8,128)} fusion(f32[80,1280]{0,1:T(8,128)} %scatter_custom_fusion.2, s32[3072]{0:T(1024)} %bitcast.266, f32[]{:T(128)} %constant.24.clone.8, f32[3072]{0:T(1024)S(1)} %copy-done.1, pred[3072]{0:T(1024)(128)(4,1)S(1)} %compare_and_fusion.1, f32[80,1280]{0,1:T(8,128)S(1)} %fusion.173, s32[3072]{0:T(1024)S(1)} %fusion.177), kind=kCustom, calls=%fused_computation.121 | custom fusion | flops 737280 | bytes 847360 | tf_op jit(solution)/shard_map/scatter-add | solution.py:98
  203.9 2.6 fusion.49
  206.5 30.0 %psum.36 = f32[16,20]{1,0:T(8,128)S(1)} all-reduce(f32[16,20]{1,0:T(8,128)S(1)} %fusion.49), channel_id=1, replica_groups=mesh['group'=2,'cell'=16] {'cell'}, use_global_device_ids=true, to_apply=%region_7.12 | all-reduce | flops 320 | bytes 2560 | tf_op jit(solution)/shard_map/psum | solution.py:39
  240.9 4.4 collective-permute-done.2
  247.9 26.6 %scatter_custom_fusion.4 = f32[80,1280]{0,1:T(8,128)} fusion(s32[3072]{0:T(1024)} %bitcast.275, f32[]{:T(128)} %constant.24.clone.8, f32[3072]{0:T(1024)S(1)} %copy-done.1, pred[3072]{0:T(1024)(128)(4,1)S(1)} %compare_and_fusion, f32[]{:T(128)} %constant.44.clone.1, f32[80,1280]{0,1:T(8,128)S(1)} %fusion.170, s32[3072]{0:T(1024)S(1)} %fusion.178), kind=kCustom, calls=%fused_computation.118 | custom fusion | flops 737280 | bytes 847872 | tf_op jit(solution)/shard_map/scatter-add | solution.py:95
  276.6 27.8 %scatter_custom_fusion.5 = f32[80,1280]{0,1:T(8,128)} fusion(f32[80,1280]{0,1:T(8,128)} %scatter_custom_fusion.4, s32[3072]{0:T(1024)} %bitcast.267, f32[]{:T(128)} %constant.24.clone.8, f32[3072]{0:T(1024)S(1)} %copy-done.1, pred[3072]{0:T(1024)(128)(4,1)S(1)} %compare_and_fusion.1, f32[80,1280]{0,1:T(8,128)S(1)} %fusion.169, s32[3072]{0:T(1024)S(1)} %fusion.177), kind=kCustom, calls=%fused_computation.115 | custom fusion | flops 737280 | bytes 847360 | tf_op jit(solution)/shard_map/scatter-add | solution.py:98
  316.4 2.1 fusion.172
  318.5 37.3 %scatter_custom_fusion.6 = f32[80,1280]{0,1:T(8,128)} fusion(s32[3072]{0:T(1024)} %bitcast.276, f32[]{:T(128)} %constant.24.clone.8, f32[3072]{0:T(1024)S(1)} %copy-done.1, pred[3072]{0:T(1024)(128)(4,1)S(1)} %compare_and_fusion, f32[]{:T(128)} %constant.44.clone.1, f32[80,1280]{0,1:T(8,128)} %fusion.172, s32[3072]{0:T(1024)S(1)} %fusion.178), kind=kCustom, calls=%fused_computation.112 | custom fusion | flops 737280 | bytes 1093632 | tf_op jit(solution)/shard_map/scatter-add | solution.py:95
  355.8 2.1 fusion.171
  357.9 38.6 %scatter_custom_fusion.7 = f32[80,1280]{0,1:T(8,128)} fusion(f32[80,1280]{0,1:T(8,128)} %scatter_custom_fusion.6, s32[3072]{0:T(1024)} %bitcast.268, f32[]{:T(128)} %constant.24.clone.8, f32[3072]{0:T(1024)S(1)} %copy-done.1, pred[3072]{0:T(1024)(128)(4,1)S(1)} %compare_and_fusion.1, f32[80,1280]{0,1:T(8,128)} %fusion.171, s32[3072]{0:T(1024)S(1)} %fusion.177), kind=kCustom, calls=%fused_computation.109 | custom fusion | flops 737280 | bytes 1093120 | tf_op jit(solution)/shard_map/scatter-add | solution.py:98
  411.0 2.6 fusion.50
  413.6 30.0 %psum.37 = f32[16,20]{1,0:T(8,128)S(1)} all-reduce(f32[16,20]{1,0:T(8,128)S(1)} %fusion.50), channel_id=1, replica_groups=mesh['group'=2,'cell'=16] {'cell'}, use_global_device_ids=true, to_apply=%region_13.18 | all-reduce | flops 320 | bytes 2560 | tf_op jit(solution)/shard_map/psum | solution.py:39
  448.1 4.0 collective-permute-done.4
  454.7 27.0 %scatter_custom_fusion.8 = f32[80,1280]{0,1:T(8,128)} fusion(s32[3072]{0:T(1024)} %bitcast.277, f32[]{:T(128)} %constant.24.clone.8, f32[3072]{0:T(1024)S(1)} %copy-done.1, pred[3072]{0:T(1024)(128)(4,1)S(1)} %compare_and_fusion, f32[]{:T(128)} %constant.44.clone.1, f32[80,1280]{0,1:T(8,128)S(1)} %fusion.166, s32[3072]{0:T(1024)S(1)} %fusion.178), kind=kCustom, calls=%fused_computation.106 | custom fusion | flops 737280 | bytes 847872 | tf_op jit(solution)/shard_map/scatter-add | solution.py:95
  483.7 27.7 %scatter_custom_fusion.9 = f32[80,1280]{0,1:T(8,128)} fusion(f32[80,1280]{0,1:T(8,128)} %scatter_custom_fusion.8, s32[3072]{0:T(1024)} %bitcast.269, f32[]{:T(128)} %constant.24.clone.8, f32[3072]{0:T(1024)S(1)} %copy-done.1, pred[3072]{0:T(1024)(128)(4,1)S(1)} %compare_and_fusion.1, f32[80,1280]{0,1:T(8,128)S(1)} %fusion.165, s32[3072]{0:T(1024)S(1)} %fusion.177), kind=kCustom, calls=%fused_computation.103 | custom fusion | flops 737280 | bytes 847360 | tf_op jit(solution)/shard_map/scatter-add | solution.py:98
  523.4 2.1 fusion.168
  525.5 37.5 %scatter_custom_fusion.10 = f32[80,1280]{0,1:T(8,128)} fusion(s32[3072]{0:T(1024)} %bitcast.278, f32[]{:T(128)} %constant.24.clone.8, f32[3072]{0:T(1024)S(1)} %copy-done.1, pred[3072]{0:T(1024)(128)(4,1)S(1)} %compare_and_fusion, f32[]{:T(128)} %constant.44.clone.1, f32[80,1280]{0,1:T(8,128)} %fusion.168, s32[3072]{0:T(1024)S(1)} %fusion.178), kind=kCustom, calls=%fused_computation.100 | custom fusion | flops 737280 | bytes 1093632 | tf_op jit(solution)/shard_map/scatter-add | solution.py:95
  563.0 2.1 fusion.167
  565.0 38.4 %scatter_custom_fusion.11 = f32[80,1280]{0,1:T(8,128)} fusion(f32[80,1280]{0,1:T(8,128)} %scatter_custom_fusion.10, s32[3072]{0:T(1024)} %bitcast.270, f32[]{:T(128)} %constant.24.clone.8, f32[3072]{0:T(1024)S(1)} %copy-done.1, pred[3072]{0:T(1024)(128)(4,1)S(1)} %compare_and_fusion.1, f32[80,1280]{0,1:T(8,128)} %fusion.167, s32[3072]{0:T(1024)S(1)} %fusion.177), kind=kCustom, calls=%fused_computation.97 | custom fusion | flops 737280 | bytes 1093120 | tf_op jit(solution)/shard_map/scatter-add | solution.py:98
  617.9 2.6 fusion.51
  620.5 30.4 %psum.38 = f32[16,20]{1,0:T(8,128)S(1)} all-reduce(f32[16,20]{1,0:T(8,128)S(1)} %fusion.51), channel_id=1, replica_groups=mesh['group'=2,'cell'=16] {'cell'}, use_global_device_ids=true, to_apply=%region_19.24 | all-reduce | flops 320 | bytes 2560 | tf_op jit(solution)/shard_map/psum | solution.py:39
  654.8 4.8 collective-permute-done.6
  661.5 26.0 %scatter_custom_fusion.12 = f32[80,1280]{0,1:T(8,128)S(1)} fusion(s32[3072]{0:T(1024)} %bitcast.279, f32[]{:T(128)} %constant.24.clone.8, f32[3072]{0:T(1024)S(1)} %copy-done.1, pred[3072]{0:T(1024)(128)(4,1)S(1)} %compare_and_fusion, f32[]{:T(128)} %constant.44.clone.1, f32[80,1280]{0,1:T(8,128)S(1)} %fusion.162, s32[3072]{0:T(1024)S(1)} %fusion.178), kind=kCustom, calls=%fused_computation.94 | custom fusion | flops 737280 | bytes 847872 | tf_op jit(solution)/shard_map/scatter-add | solution.py:95
  688.7 26.3 %scatter_custom_fusion.13 = f32[80,1280]{0,1:T(8,128)S(1)} fusion(f32[80,1280]{0,1:T(8,128)S(1)} %scatter_custom_fusion.12, s32[3072]{0:T(1024)} %bitcast.271, f32[]{:T(128)} %constant.24.clone.8, f32[3072]{0:T(1024)S(1)} %copy-done.1, pred[3072]{0:T(1024)(128)(4,1)S(1)} %compare_and_fusion.1, f32[80,1280]{0,1:T(8,128)S(1)} %fusion.161, s32[3072]{0:T(1024)S(1)} %fusion.177), kind=kCustom, calls=%fused_computation.91 | custom fusion | flops 737280 | bytes 1093120 | tf_op jit(solution)/shard_map/scatter-add | solution.py:98
  723.8 26.6 %scatter_custom_fusion.14 = f32[80,1280]{0,1:T(8,128)} fusion(s32[3072]{0:T(1024)} %bitcast.280, f32[]{:T(128)} %constant.24.clone.8, f32[3072]{0:T(1024)S(1)} %copy-done.1, pred[3072]{0:T(1024)(128)(4,1)S(1)} %compare_and_fusion, f32[]{:T(128)} %constant.44.clone.1, f32[80,1280]{0,1:T(8,128)S(1)} %fusion.164, s32[3072]{0:T(1024)S(1)} %fusion.178), kind=kCustom, calls=%fused_computation.88 | custom fusion | flops 737280 | bytes 847872 | tf_op jit(solution)/shard_map/scatter-add | solution.py:95
  751.6 27.9 %scatter_custom_fusion.15 = f32[80,1280]{0,1:T(8,128)} fusion(f32[80,1280]{0,1:T(8,128)} %scatter_custom_fusion.14, s32[3072]{0:T(1024)} %bitcast.272, f32[]{:T(128)} %constant.24.clone.8, f32[3072]{0:T(1024)S(1)} %copy-done.1, pred[3072]{0:T(1024)(128)(4,1)S(1)} %compare_and_fusion.1, f32[80,1280]{0,1:T(8,128)S(1)} %fusion.163, s32[3072]{0:T(1024)S(1)} %fusion.177), kind=kCustom, calls=%fused_computation.85 | custom fusion | flops 737280 | bytes 847360 | tf_op jit(solution)/shard_map/scatter-add | solution.py:98
  790.0 30.8 %psum.39 = f32[16,20]{1,0:T(8,128)} all-reduce(f32[16,20]{1,0:T(8,128)S(1)} %fusion.52), channel_id=1, replica_groups=mesh['group'=2,'cell'=16] {'cell'}, use_global_device_ids=true, to_apply=%region_25.30 | all-reduce | flops 320 | bytes 2560 | tf_op jit(solution)/shard_map/psum | solution.py:39
  (302 shorter events, 151.8 us)
Async XLA Ops:
  0.6 9.1 %copy-start.24 = (s32[2,3072]{1,0:T(2,128)S(1)}, s32[2,3072]{1,0:T(2,128)}, u32[]{:S(2)}) copy-start(s32[2,3072]{1,0:T(2,128)} %param.32) | copy-start | bytes 73732
  0.6 10.0 %copy-start.23 = (f32[16,5,1024]{2,0,1:T(8,128)S(1)}, f32[16,5,1024]{2,0,1:T(8,128)}, u32[]{:S(2)}) copy-start(f32[16,5,1024]{2,0,1:T(8,128)} %param.27) | copy-start | bytes 983044
  1.4 7.6 copy-start.31
  1.4 7.6 copy-start.35
  1.4 7.6 copy-start.36
  2.2 8.7 %copy-start = (f32[20,5,1024]{2,0,1:T(8,128)S(1)}, f32[20,5,1024]{2,0,1:T(8,128)}, u32[]{:S(2)}) copy-start(f32[20,5,1024]{2,0,1:T(8,128)} %param.30) | copy-start | bytes 1228804
  2.9 59.0 %collective-permute-start.1 = (f32[80,128]{1,0:T(8,128)}, f32[80,128]{1,0:T(8,128)S(1)}, u32[]{:S(2)}, u32[]{:S(2)}) collective-permute-start(f32[80,128]{1,0:T(8,128)} %select_bitcast_fusion.6), channel_id=1, source_target_pairs={{0,15},{1,0},{2,1},{3,2},{4,3},{5,4},{6,5},{7,6},{8,7},{9,8},{10,9... | collective-permute-start | bytes 122888 | tf_op jit(solution)/shard_map/ppermute | solution.py:14
  9.7 52.2 %collective-permute-start = (f32[80,128]{1,0:T(8,128)}, f32[80,128]{1,0:T(8,128)S(1)}, u32[]{:S(2)}, u32[]{:S(2)}) collective-permute-start(f32[80,128]{1,0:T(8,128)} %select_bitcast_fusion.7), channel_id=1, source_target_pairs={{0,1},{1,2},{2,3},{3,4},{4,5},{5,6},{6,7},{7,8},{8,9},{9,10},{10,1... | collective-permute-start | bytes 122888 | tf_op jit(solution)/shard_map/ppermute | solution.py:14
  10.8 36.4 %copy-start.38 = (f32[20]{0:T(128)S(1)}, f32[20]{0:T(128)}, u32[]{:S(2)}) copy-start(f32[20]{0:T(128)} %param.31) | copy-start | bytes 244
  47.4 3.4 copy-start.45
  47.4 3.4 copy-start.44
  47.6 3.9 copy-start.42
  61.1 4.0 copy-start.1
  201.5 35.0 %copy-start.39 = (f32[20]{0:T(128)S(1)}, f32[20]{0:T(128)}, u32[]{:S(2)}) copy-start(f32[20]{0:T(128)} %param.31) | copy-start | bytes 244
  203.8 34.9 %copy-start.32 = (pred[128]{0:T(512)(128)(4,1)S(1)}, pred[128]{0:T(512)(128)(4,1)}, u32[]{:S(2)}) copy-start(pred[128]{0:T(512)(128)(4,1)} %copy-done.31) | copy-start | bytes 388
  238.6 1.7 collective-permute-start.3
  238.8 6.6 collective-permute-start.2
  316.4 39.4 %copy-start.13 = (f32[80,128]{1,0:T(8,128)S(1)}, f32[80,128]{1,0:T(8,128)}, u32[]{:S(2)}) copy-start(f32[80,128]{1,0:T(8,128)} %copy-done.11) | copy-start | bytes 122884
  316.4 39.4 %copy-start.19 = (f32[80,128]{1,0:T(8,128)S(1)}, f32[80,128]{1,0:T(8,128)}, u32[]{:S(2)}) copy-start(f32[80,128]{1,0:T(8,128)} %copy-done.17) | copy-start | bytes 122884
  408.6 35.0 %copy-start.40 = (f32[20]{0:T(128)S(1)}, f32[20]{0:T(128)}, u32[]{:S(2)}) copy-start(f32[20]{0:T(128)} %param.31) | copy-start | bytes 244
  411.0 34.9 %copy-start.33 = (pred[128]{0:T(512)(128)(4,1)S(1)}, pred[128]{0:T(512)(128)(4,1)}, u32[]{:S(2)}) copy-start(pred[128]{0:T(512)(128)(4,1)} %copy-done.31) | copy-start | bytes 388
  445.8 1.7 collective-permute-start.5
  445.9 6.2 collective-permute-start.4
  523.4 39.5 %copy-start.16 = (f32[80,128]{1,0:T(8,128)S(1)}, f32[80,128]{1,0:T(8,128)}, u32[]{:S(2)}) copy-start(f32[80,128]{1,0:T(8,128)} %copy-done.14) | copy-start | bytes 122884
  523.4 39.5 %copy-start.22 = (f32[80,128]{1,0:T(8,128)S(1)}, f32[80,128]{1,0:T(8,128)}, u32[]{:S(2)}) copy-start(f32[80,128]{1,0:T(8,128)} %copy-done.20) | copy-start | bytes 122884
  615.5 35.4 %copy-start.41 = (f32[20]{0:T(128)S(1)}, f32[20]{0:T(128)}, u32[]{:S(2)}) copy-start(f32[20]{0:T(128)} %param.31) | copy-start | bytes 244
  617.9 35.3 %copy-start.34 = (pred[128]{0:T(512)(128)(4,1)S(1)}, pred[128]{0:T(512)(128)(4,1)}, u32[]{:S(2)}) copy-start(pred[128]{0:T(512)(128)(4,1)} %copy-done.31) | copy-start | bytes 388
  653.1 1.7 collective-permute-start.7
  653.2 6.4 collective-permute-start.6
  654.8 4.8 copy-start.7
  661.4 26.0 %copy-start.8 = (f32[80,128]{1,0:T(8,128)S(1)}, f32[80,128]{1,0:T(8,128)}, u32[]{:S(2)}) copy-start(f32[80,128]{1,0:T(8,128)} %copy-done.7) | copy-start | bytes 122884
  661.5 26.0 %copy-start.10 = (f32[80,128]{1,0:T(8,128)S(1)}, f32[80,128]{1,0:T(8,128)}, u32[]{:S(2)}) copy-start(f32[80,128]{1,0:T(8,128)} %copy-done.9) | copy-start | bytes 122884
  (29 other events, 44.6 us)
where the time goes:
time: 833 us; the launch traced here: 821 us
  other arithmetic  498 us (60%)
  blocking collectives  156 us (19%)
  local copies, waits for them, and re-layouts  96.2 us (12%)
  matrix products  47.3 us (6%)
  waiting for transfers between devices  14.2 us (2%)
    scatter-add x8, other arithmetic, local(): total.at[:, left_cells]  242 us
    scatter-add x8, other arithmetic, local(): total.at[:, right_cells]  235 us
    psum x5, blocking collectives, modal_total(): return lax.psum(local_part, 'cell')  156 us
    gather x32, local copies, waits for them, and re-layouts, local(): jnp.take(resid, source_rows[var], axis=0)  43.6 us
    dot_general x28, matrix products, wide_dot(): jnp.dot(left, right, precision=lax.Precision.HIGHEST, preferred_element_t...  36.4 us
  transfers between devices with their start and end apart: 8, of which 6 were waited for; matrix products, arithmetic and copies ran while one was open for 2% of the time, Pallas kernels for 0%

commit v1 on v0

--- a/solution.py
+++ b/solution.py
@@ -7,6 +7,12 @@
 
 ITERS = 4
 frequency = 0.04
+
+
+def summed_here(x, axis):
+    parts = lax.all_gather(x, axis, axis=0, tiled=False)
+    total = parts.sum(axis=0)
+    return total
 
 
 def from_behind(value, axis, by):
@@ -36,7 +42,7 @@
         preferred_element_type=jnp.float32,
     )
     local_part = jnp.einsum("ivmv->im", gram.reshape(count, nvar, modes, nvar))
-    return lax.psum(local_part, "cell")
+    return summed_here(local_part, "cell")
 
 
 def local(

time: 833 us -> 772 us (0.927)
  blocking collectives: 156 us -> 89.5 us
    psum x5 -> x0, blocking collectives: 156 us -> none  [modal_total(): return lax.psum(local_part, 'cell')]
    all_gather x0 -> x5, blocking collectives: none -> 89.5 us  [summed_here(): parts = lax.all_gather(x, axis, axis=0, tiled=False)]
  transfers between devices with their start and end apart: 8 -> 8, of which waited for: 6 -> 6; matrix products, arithmetic and copies ran while one was open for 2% -> 3% of each run, Pallas kernels for 0% -> 0%
where the time goes in v1:
time: 772 us; the launch traced here: 760 us
  other arithmetic  498 us (65%)
  local copies, waits for them, and re-layouts  96.2 us (12%)
  blocking collectives  89.5 us (12%)
  matrix products  47.3 us (6%)
  waiting for transfers between devices  15.7 us (2%)
  starting transfers between devices  11 us (1%)
    scatter-add x8, other arithmetic, local(): total.at[:, left_cells]  242 us
    scatter-add x8, other arithmetic, local(): total.at[:, right_cells]  235 us
    all_gather x5, blocking collectives, summed_here(): parts = lax.all_gather(x, axis, axis=0, tiled=False)  89.5 us
    gather x32, local copies, waits for them, and re-layouts, local(): jnp.take(resid, source_rows[var], axis=0)  43.6 us
    dot_general x28, matrix products, wide_dot(): jnp.dot(left, right, precision=lax.Precision.HIGHEST, preferred_element_t...  36.4 us
    ppermute x8, waiting for transfers between devices, from_behind(): lax.ppermute(value, axis, [(i, (i + by) % devices) for i in range(devices)])  15.7 us
  transfers between devices with their start and end apart: 8, of which 6 were waited for; matrix products, arithmetic and copies ran while one was open for 3% of the time, Pallas kernels for 0%

profile of v1, /device:TPU:0, one launch (start us, length us, event | category | flops | bytes accessed | tf_op | source)
XLA Modules:
  0.0 760.4 jit_solution(7187127222050761681)
XLA Ops:
  2.9 5.4 collective-permute-start.1
  12.7 18.5 %all-gather = f32[256,20]{1,0:T(8,128)S(1)} all-gather(f32[16,20]{1,0:T(8,128)S(1)} %fusion.48), channel_id=2, replica_groups=mesh['group'=2,'cell'=16] {'cell'}, dimensions={0}, use_global_device_ids=true | all-gather | bytes 21760 | tf_op jit(solution)/shard_map/all_gather | solution.py:13
  49.2 26.8 %scatter_custom_fusion = f32[80,1280]{0,1:T(8,128)} fusion(s32[3072]{0:T(1024)} %bitcast.283, f32[]{:T(128)} %constant.24.clone.8, f32[3072]{0:T(1024)S(1)} %copy-done.1, pred[3072]{0:T(1024)(128)(4,1)S(1)} %compare_and_fusion, f32[]{:T(128)} %constant.44.clone.1, f32[80,1280]{0,1:T(8,128)S(1)} %fusion.107, s32[3072]{0:T(1024)S(1)} %fusion.178), kind=kCustom, calls=%fused_computation.130 | custom fusion | flops 737280 | bytes 847872 | tf_op jit(solution)/shard_map/scatter-add | solution.py:101
  78.0 27.7 %scatter_custom_fusion.1 = f32[80,1280]{0,1:T(8,128)} fusion(f32[80,1280]{0,1:T(8,128)} %scatter_custom_fusion, s32[3072]{0:T(1024)} %bitcast.275, f32[]{:T(128)} %constant.24.clone.8, f32[3072]{0:T(1024)S(1)} %copy-done.1, pred[3072]{0:T(1024)(128)(4,1)S(1)} %compare_and_fusion.1, f32[80,1280]{0,1:T(8,128)S(1)} %fusion.106, s32[3072]{0:T(1024)S(1)} %fusion.177), kind=kCustom, calls=%fused_computation.127 | custom fusion | flops 737280 | bytes 847360 | tf_op jit(solution)/shard_map/scatter-add | solution.py:104
  116.2 26.8 %scatter_custom_fusion.2 = f32[80,1280]{0,1:T(8,128)} fusion(s32[3072]{0:T(1024)} %bitcast.284, f32[]{:T(128)} %constant.24.clone.8, f32[3072]{0:T(1024)S(1)} %copy-done.1, pred[3072]{0:T(1024)(128)(4,1)S(1)} %compare_and_fusion, f32[]{:T(128)} %constant.44.clone.1, f32[80,1280]{0,1:T(8,128)S(1)} %fusion.174, s32[3072]{0:T(1024)S(1)} %fusion.178), kind=kCustom, calls=%fused_computation.124 | custom fusion | flops 737280 | bytes 847872 | tf_op jit(solution)/shard_map/scatter-add | solution.py:101
  145.0 27.7 %scatter_custom_fusion.3 = f32[80,1280]{0,1:T(8,128)} fusion(f32[80,1280]{0,1:T(8,128)} %scatter_custom_fusion.2, s32[3072]{0:T(1024)} %bitcast.276, f32[]{:T(128)} %constant.24.clone.8, f32[3072]{0:T(1024)S(1)} %copy-done.1, pred[3072]{0:T(1024)(128)(4,1)S(1)} %compare_and_fusion.1, f32[80,1280]{0,1:T(8,128)S(1)} %fusion.173, s32[3072]{0:T(1024)S(1)} %fusion.177), kind=kCustom, calls=%fused_computation.121 | custom fusion | flops 737280 | bytes 847360 | tf_op jit(solution)/shard_map/scatter-add | solution.py:104
  187.8 2.6 fusion.49
  190.5 18.5 %all-gather.1 = f32[256,20]{1,0:T(8,128)S(1)} all-gather(f32[16,20]{1,0:T(8,128)S(1)} %fusion.49), channel_id=3, replica_groups=mesh['group'=2,'cell'=16] {'cell'}, dimensions={0}, use_global_device_ids=true | all-gather | bytes 21760 | tf_op jit(solution)/shard_map/all_gather | solution.py:13
  214.4 4.4 collective-permute-done.2
  221.4 26.6 %scatter_custom_fusion.4 = f32[80,1280]{0,1:T(8,128)} fusion(s32[3072]{0:T(1024)} %bitcast.285, f32[]{:T(128)} %constant.24.clone.8, f32[3072]{0:T(1024)S(1)} %copy-done.1, pred[3072]{0:T(1024)(128)(4,1)S(1)} %compare_and_fusion, f32[]{:T(128)} %constant.44.clone.1, f32[80,1280]{0,1:T(8,128)S(1)} %fusion.170, s32[3072]{0:T(1024)S(1)} %fusion.178), kind=kCustom, calls=%fused_computation.118 | custom fusion | flops 737280 | bytes 847872 | tf_op jit(solution)/shard_map/scatter-add | solution.py:101
  250.0 27.8 %scatter_custom_fusion.5 = f32[80,1280]{0,1:T(8,128)} fusion(f32[80,1280]{0,1:T(8,128)} %scatter_custom_fusion.4, s32[3072]{0:T(1024)} %bitcast.277, f32[]{:T(128)} %constant.24.clone.8, f32[3072]{0:T(1024)S(1)} %copy-done.1, pred[3072]{0:T(1024)(128)(4,1)S(1)} %compare_and_fusion.1, f32[80,1280]{0,1:T(8,128)S(1)} %fusion.169, s32[3072]{0:T(1024)S(1)} %fusion.177), kind=kCustom, calls=%fused_computation.115 | custom fusion | flops 737280 | bytes 847360 | tf_op jit(solution)/shard_map/scatter-add | solution.py:104
  289.9 2.1 fusion.172
  291.9 37.3 %scatter_custom_fusion.6 = f32[80,1280]{0,1:T(8,128)} fusion(s32[3072]{0:T(1024)} %bitcast.286, f32[]{:T(128)} %constant.24.clone.8, f32[3072]{0:T(1024)S(1)} %copy-done.1, pred[3072]{0:T(1024)(128)(4,1)S(1)} %compare_and_fusion, f32[]{:T(128)} %constant.44.clone.1, f32[80,1280]{0,1:T(8,128)} %fusion.172, s32[3072]{0:T(1024)S(1)} %fusion.178), kind=kCustom, calls=%fused_computation.112 | custom fusion | flops 737280 | bytes 1093632 | tf_op jit(solution)/shard_map/scatter-add | solution.py:101
  329.3 2.1 fusion.171
  331.3 38.6 %scatter_custom_fusion.7 = f32[80,1280]{0,1:T(8,128)} fusion(f32[80,1280]{0,1:T(8,128)} %scatter_custom_fusion.6, s32[3072]{0:T(1024)} %bitcast.278, f32[]{:T(128)} %constant.24.clone.8, f32[3072]{0:T(1024)S(1)} %copy-done.1, pred[3072]{0:T(1024)(128)(4,1)S(1)} %compare_and_fusion.1, f32[80,1280]{0,1:T(8,128)} %fusion.171, s32[3072]{0:T(1024)S(1)} %fusion.177), kind=kCustom, calls=%fused_computation.109 | custom fusion | flops 737280 | bytes 1093120 | tf_op jit(solution)/shard_map/scatter-add | solution.py:104
  384.4 2.6 fusion.50
  387.0 17.5 %all-gather.2 = f32[256,20]{1,0:T(8,128)S(1)} all-gather(f32[16,20]{1,0:T(8,128)S(1)} %fusion.50), channel_id=4, replica_groups=mesh['group'=2,'cell'=16] {'cell'}, dimensions={0}, use_global_device_ids=true | all-gather | bytes 21760 | tf_op jit(solution)/shard_map/all_gather | solution.py:13
  410.9 4.0 collective-permute-done.4
  417.5 27.0 %scatter_custom_fusion.8 = f32[80,1280]{0,1:T(8,128)} fusion(s32[3072]{0:T(1024)} %bitcast.287, f32[]{:T(128)} %constant.24.clone.8, f32[3072]{0:T(1024)S(1)} %copy-done.1, pred[3072]{0:T(1024)(128)(4,1)S(1)} %compare_and_fusion, f32[]{:T(128)} %constant.44.clone.1, f32[80,1280]{0,1:T(8,128)S(1)} %fusion.166, s32[3072]{0:T(1024)S(1)} %fusion.178), kind=kCustom, calls=%fused_computation.106 | custom fusion | flops 737280 | bytes 847872 | tf_op jit(solution)/shard_map/scatter-add | solution.py:101
  446.5 27.7 %scatter_custom_fusion.9 = f32[80,1280]{0,1:T(8,128)} fusion(f32[80,1280]{0,1:T(8,128)} %scatter_custom_fusion.8, s32[3072]{0:T(1024)} %bitcast.279, f32[]{:T(128)} %constant.24.clone.8, f32[3072]{0:T(1024)S(1)} %copy-done.1, pred[3072]{0:T(1024)(128)(4,1)S(1)} %compare_and_fusion.1, f32[80,1280]{0,1:T(8,128)S(1)} %fusion.165, s32[3072]{0:T(1024)S(1)} %fusion.177), kind=kCustom, calls=%fused_computation.103 | custom fusion | flops 737280 | bytes 847360 | tf_op jit(solution)/shard_map/scatter-add | solution.py:104
  486.2 2.1 fusion.168
  488.3 37.5 %scatter_custom_fusion.10 = f32[80,1280]{0,1:T(8,128)} fusion(s32[3072]{0:T(1024)} %bitcast.288, f32[]{:T(128)} %constant.24.clone.8, f32[3072]{0:T(1024)S(1)} %copy-done.1, pred[3072]{0:T(1024)(128)(4,1)S(1)} %compare_and_fusion, f32[]{:T(128)} %constant.44.clone.1, f32[80,1280]{0,1:T(8,128)} %fusion.168, s32[3072]{0:T(1024)S(1)} %fusion.178), kind=kCustom, calls=%fused_computation.100 | custom fusion | flops 737280 | bytes 1093632 | tf_op jit(solution)/shard_map/scatter-add | solution.py:101
  525.8 2.1 fusion.167
  527.8 38.4 %scatter_custom_fusion.11 = f32[80,1280]{0,1:T(8,128)} fusion(f32[80,1280]{0,1:T(8,128)} %scatter_custom_fusion.10, s32[3072]{0:T(1024)} %bitcast.280, f32[]{:T(128)} %constant.24.clone.8, f32[3072]{0:T(1024)S(1)} %copy-done.1, pred[3072]{0:T(1024)(128)(4,1)S(1)} %compare_and_fusion.1, f32[80,1280]{0,1:T(8,128)} %fusion.167, s32[3072]{0:T(1024)S(1)} %fusion.177), kind=kCustom, calls=%fused_computation.97 | custom fusion | flops 737280 | bytes 1093120 | tf_op jit(solution)/shard_map/scatter-add | solution.py:104
  580.7 2.6 fusion.51
  583.3 17.5 %all-gather.3 = f32[256,20]{1,0:T(8,128)S(1)} all-gather(f32[16,20]{1,0:T(8,128)S(1)} %fusion.51), channel_id=5, replica_groups=mesh['group'=2,'cell'=16] {'cell'}, dimensions={0}, use_global_device_ids=true | all-gather | bytes 21760 | tf_op jit(solution)/shard_map/all_gather | solution.py:13
  606.6 4.8 collective-permute-done.6
  613.3 26.0 %scatter_custom_fusion.12 = f32[80,1280]{0,1:T(8,128)S(1)} fusion(s32[3072]{0:T(1024)} %bitcast.289, f32[]{:T(128)} %constant.24.clone.8, f32[3072]{0:T(1024)S(1)} %copy-done.1, pred[3072]{0:T(1024)(128)(4,1)S(1)} %compare_and_fusion, f32[]{:T(128)} %constant.44.clone.1, f32[80,1280]{0,1:T(8,128)S(1)} %fusion.162, s32[3072]{0:T(1024)S(1)} %fusion.178), kind=kCustom, calls=%fused_computation.94 | custom fusion | flops 737280 | bytes 847872 | tf_op jit(solution)/shard_map/scatter-add | solution.py:101
  640.5 26.3 %scatter_custom_fusion.13 = f32[80,1280]{0,1:T(8,128)S(1)} fusion(f32[80,1280]{0,1:T(8,128)S(1)} %scatter_custom_fusion.12, s32[3072]{0:T(1024)} %bitcast.281, f32[]{:T(128)} %constant.24.clone.8, f32[3072]{0:T(1024)S(1)} %copy-done.1, pred[3072]{0:T(1024)(128)(4,1)S(1)} %compare_and_fusion.1, f32[80,1280]{0,1:T(8,128)S(1)} %fusion.161, s32[3072]{0:T(1024)S(1)} %fusion.177), kind=kCustom, calls=%fused_computation.91 | custom fusion | flops 737280 | bytes 1093120 | tf_op jit(solution)/shard_map/scatter-add | solution.py:104
  675.6 26.6 %scatter_custom_fusion.14 = f32[80,1280]{0,1:T(8,128)} fusion(s32[3072]{0:T(1024)} %bitcast.290, f32[]{:T(128)} %constant.24.clone.8, f32[3072]{0:T(1024)S(1)} %copy-done.1, pred[3072]{0:T(1024)(128)(4,1)S(1)} %compare_and_fusion, f32[]{:T(128)} %constant.44.clone.1, f32[80,1280]{0,1:T(8,128)S(1)} %fusion.164, s32[3072]{0:T(1024)S(1)} %fusion.178), kind=kCustom, calls=%fused_computation.88 | custom fusion | flops 737280 | bytes 847872 | tf_op jit(solution)/shard_map/scatter-add | solution.py:101
  703.5 27.9 %scatter_custom_fusion.15 = f32[80,1280]{0,1:T(8,128)} fusion(f32[80,1280]{0,1:T(8,128)} %scatter_custom_fusion.14, s32[3072]{0:T(1024)} %bitcast.282, f32[]{:T(128)} %constant.24.clone.8, f32[3072]{0:T(1024)S(1)} %copy-done.1, pred[3072]{0:T(1024)(128)(4,1)S(1)} %compare_and_fusion.1, f32[80,1280]{0,1:T(8,128)S(1)} %fusion.163, s32[3072]{0:T(1024)S(1)} %fusion.177), kind=kCustom, calls=%fused_computation.85 | custom fusion | flops 737280 | bytes 847360 | tf_op jit(solution)/shard_map/scatter-add | solution.py:104
  741.8 17.5 %all-gather.4 = f32[256,20]{1,0:T(8,128)S(1)} all-gather(f32[16,20]{1,0:T(8,128)S(1)} %fusion.52), channel_id=6, replica_groups=mesh['group'=2,'cell'=16] {'cell'}, dimensions={0}, use_global_device_ids=true | all-gather | bytes 21760 | tf_op jit(solution)/shard_map/all_gather | solution.py:13
  (307 shorter events, 157.3 us)
Async XLA Ops:
  0.6 9.1 %copy-start.24 = (s32[2,3072]{1,0:T(2,128)S(1)}, s32[2,3072]{1,0:T(2,128)}, u32[]{:S(2)}) copy-start(s32[2,3072]{1,0:T(2,128)} %param.32) | copy-start | bytes 73732
  0.6 10.0 %copy-start.23 = (f32[16,5,1024]{2,0,1:T(8,128)S(1)}, f32[16,5,1024]{2,0,1:T(8,128)}, u32[]{:S(2)}) copy-start(f32[16,5,1024]{2,0,1:T(8,128)} %param.27) | copy-start | bytes 983044
  1.4 7.6 %copy-start.31 = (pred[128]{0:T(512)(128)(4,1)}, pred[128]{0:T(512)(128)(4,1)S(1)}, u32[]{:S(2)}) copy-start(pred[128]{0:T(512)(128)(4,1)S(1)} %get-tuple-element.12) | copy-start | bytes 388
  1.4 7.6 %copy-start.35 = (pred[128]{0:T(512)(128)(4,1)}, pred[128]{0:T(512)(128)(4,1)S(1)}, u32[]{:S(2)}) copy-start(pred[128]{0:T(512)(128)(4,1)S(1)} %get-tuple-element.26) | copy-start | bytes 388
  1.4 7.6 %copy-start.36 = (s32[1024]{0:T(1024)}, s32[1024]{0:T(1024)S(1)}, u32[]{:S(2)}) copy-start(s32[1024]{0:T(1024)S(1)} %pad_clamp_fusion.9) | copy-start | bytes 12292
  2.2 8.7 %copy-start = (f32[20,5,1024]{2,0,1:T(8,128)S(1)}, f32[20,5,1024]{2,0,1:T(8,128)}, u32[]{:S(2)}) copy-start(f32[20,5,1024]{2,0,1:T(8,128)} %param.30) | copy-start | bytes 1228804
  2.9 43.0 %collective-permute-start.1 = (f32[80,128]{1,0:T(8,128)}, f32[80,128]{1,0:T(8,128)S(1)}, u32[]{:S(2)}, u32[]{:S(2)}) collective-permute-start(f32[80,128]{1,0:T(8,128)} %select_bitcast_fusion.6), channel_id=1, source_target_pairs={{0,15},{1,0},{2,1},{3,2},{4,3},{5,4},{6,5},{7,6},{8,7},{9,8},{10,9... | collective-permute-start | bytes 122888 | tf_op jit(solution)/shard_map/ppermute | solution.py:20
  9.7 36.2 %collective-permute-start = (f32[80,128]{1,0:T(8,128)}, f32[80,128]{1,0:T(8,128)S(1)}, u32[]{:S(2)}, u32[]{:S(2)}) collective-permute-start(f32[80,128]{1,0:T(8,128)} %select_bitcast_fusion.7), channel_id=1, source_target_pairs={{0,1},{1,2},{2,3},{3,4},{4,5},{5,6},{6,7},{7,8},{8,9},{9,10},{10,1... | collective-permute-start | bytes 122888 | tf_op jit(solution)/shard_map/ppermute | solution.py:20
  10.8 20.4 %copy-start.38 = (f32[20]{0:T(128)S(1)}, f32[20]{0:T(128)}, u32[]{:S(2)}) copy-start(f32[20]{0:T(128)} %param.31) | copy-start | bytes 244
  31.4 3.4 copy-start.45
  31.4 3.4 copy-start.44
  31.6 3.9 copy-start.42
  45.1 4.0 copy-start.1
  185.5 23.5 %copy-start.39 = (f32[20]{0:T(128)S(1)}, f32[20]{0:T(128)}, u32[]{:S(2)}) copy-start(f32[20]{0:T(128)} %param.31) | copy-start | bytes 244
  190.5 21.7 %copy-start.32 = (pred[128]{0:T(512)(128)(4,1)S(1)}, pred[128]{0:T(512)(128)(4,1)}, u32[]{:S(2)}) copy-start(pred[128]{0:T(512)(128)(4,1)} %copy-done.31) | copy-start | bytes 388
  211.2 2.6 collective-permute-start.3
  212.2 6.6 collective-permute-start.2
  289.9 39.4 %copy-start.13 = (f32[80,128]{1,0:T(8,128)S(1)}, f32[80,128]{1,0:T(8,128)}, u32[]{:S(2)}) copy-start(f32[80,128]{1,0:T(8,128)} %copy-done.11) | copy-start | bytes 122884
  289.9 39.4 %copy-start.19 = (f32[80,128]{1,0:T(8,128)S(1)}, f32[80,128]{1,0:T(8,128)}, u32[]{:S(2)}) copy-start(f32[80,128]{1,0:T(8,128)} %copy-done.17) | copy-start | bytes 122884
  382.0 22.5 %copy-start.40 = (f32[20]{0:T(128)S(1)}, f32[20]{0:T(128)}, u32[]{:S(2)}) copy-start(f32[20]{0:T(128)} %param.31) | copy-start | bytes 244
  387.0 21.7 %copy-start.33 = (pred[128]{0:T(512)(128)(4,1)S(1)}, pred[128]{0:T(512)(128)(4,1)}, u32[]{:S(2)}) copy-start(pred[128]{0:T(512)(128)(4,1)} %copy-done.31) | copy-start | bytes 388
  406.7 3.6 collective-permute-start.5
  408.7 6.2 collective-permute-start.4
  486.2 39.5 %copy-start.16 = (f32[80,128]{1,0:T(8,128)S(1)}, f32[80,128]{1,0:T(8,128)}, u32[]{:S(2)}) copy-start(f32[80,128]{1,0:T(8,128)} %copy-done.14) | copy-start | bytes 122884
  486.2 39.5 %copy-start.22 = (f32[80,128]{1,0:T(8,128)S(1)}, f32[80,128]{1,0:T(8,128)}, u32[]{:S(2)}) copy-start(f32[80,128]{1,0:T(8,128)} %copy-done.20) | copy-start | bytes 122884
  578.4 22.5 %copy-start.41 = (f32[20]{0:T(128)S(1)}, f32[20]{0:T(128)}, u32[]{:S(2)}) copy-start(f32[20]{0:T(128)} %param.31) | copy-start | bytes 244
  583.3 21.7 %copy-start.34 = (pred[128]{0:T(512)(128)(4,1)S(1)}, pred[128]{0:T(512)(128)(4,1)}, u32[]{:S(2)}) copy-start(pred[128]{0:T(512)(128)(4,1)} %copy-done.31) | copy-start | bytes 388
  603.0 3.6 collective-permute-start.7
  605.1 6.4 collective-permute-start.6
  606.6 4.8 copy-start.7
  613.3 26.0 %copy-start.8 = (f32[80,128]{1,0:T(8,128)S(1)}, f32[80,128]{1,0:T(8,128)}, u32[]{:S(2)}) copy-start(f32[80,128]{1,0:T(8,128)} %copy-done.7) | copy-start | bytes 122884
  613.3 26.0 %copy-start.10 = (f32[80,128]{1,0:T(8,128)S(1)}, f32[80,128]{1,0:T(8,128)}, u32[]{:S(2)}) copy-start(f32[80,128]{1,0:T(8,128)} %copy-done.9) | copy-start | bytes 122884
  (29 other events, 44.6 us)
